TPU v7x, 32 devices: a whole 2x2x4 slice. The times are simulated.
32 devices in a mesh: gx: 16 (over z, y, core), gy: 2 (over x).
Axes of the slice: x: 2, y: 2, z: 4, core: 2. Of those that a mesh axis runs over, the one named last changes fastest.
Arguments:
- conserved: float32 [5, 16, 128, 256], P(None, None, 'gx', 'gy'), may hold values from -2.5 to 9, as said below
- register: float32 [5, 16, 128, 256], P(None, None, 'gx', 'gy'), may hold values from -1 to 1, as said below
- ghost_planes: float32 [5, 16, 128, 256], P(None, None, 'gx', 'gy'), may hold values from -2.5 to 9, as said below
Outputs:
- advanced: float32 [5, 16, 128, 256], P(None, None, 'gx', 'gy')
- carried: float32 [5, 16, 128, 256], P(None, None, 'gx', 'gy')
Inputs may be any that keep to these rules, and one draw needn't show every extreme that they name: `conserved`: every cell holds density in [0.6, 1.4], velocity components of magnitude at most 1.5 and T = 1.4 p / rho in [0.7, 1.4]; energy is E = p / 0.4 + 0.5 rho |u|^2. `ghost_planes`: every cell holds density in [0.6, 1.4], velocity components of magnitude at most 1.5 and T = 1.4 p / rho in [0.7, 1.4]; energy is E = p / 0.4 + 0.5 rho |u|^2. `register`: the density row lies in [-0.25, 0.25]; the momentum and energy rows lie in [-1, 1]. Density stays at 0.3 or more through both sections.
All inputs are finite; a program needn't handle non-finite values.
Results may differ from a plain program's by a relative error of at most 0.00002.
Values sent between devices are 32-bit elements; how exact they have to be, the bound alone decides.
A program may use at most 64 MiB of HBM per device.

v0:
```python
import functools

import jax
import jax.numpy as jnp
from jax import lax
from jax.experimental import pallas as pl
from jax.experimental.pallas import tpu as pltpu
from jax.sharding import PartitionSpec as P

MESH = pl.DeviceIdType.MESH

viscosity = 0.15
conductivity = 0.15 / (0.4 * 0.7)
time_step = 0.2
section_a = (-0.41789047, -1.19215169)
section_b = (0.37921031, 0.82295503)
stencil = (0.8, -0.2, 4.0 / 105.0, -1.0 / 280.0)
CH = 4
HALF = CH // 2
Y_STATE = (4 * CH + 15) // 16
Y_FLUX = (5 * CH + 15) // 16


def kernel(
    nx,
    ny,
    chunks,
    cons_hbm,
    reg_hbm,
    ghost_hbm,
    state_out,
    register_out,
    slope_out,
    QE,
    PR,
    REG,
    FX,
    FY,
    FZ,
    GH,
    DX,
    DY,
    DZ,
    SL,
    XS,
    XR,
    YS,
    YR,
    XSG,
    XRG,
    YSG,
    YRG,
    in_sem,
    xs_sem,
    xr_sem,
    ys_sem,
    yr_sem,
    gs_sem,
    gr_sem,
):
    ix = lax.axis_index("gx")
    iy = lax.axis_index("gy")
    right = lax.rem(ix + 1, nx)
    left = lax.rem(ix + nx - 1, nx)
    up = lax.rem(iy + 1, ny)
    down = lax.rem(iy + ny - 1, ny)
    y_sides = (0,) if ny == 2 else (0, 1)

    planes = chunks * CH
    ghost = ghost_hbm.shape[1] // 2
    loads = [
        pltpu.make_async_copy(cons_hbm, QE.at[:, pl.ds(ghost, planes)], in_sem.at[0]),
        pltpu.make_async_copy(ghost_hbm.at[:, pl.ds(0, ghost)], QE.at[:, pl.ds(0, ghost)], in_sem.at[1]),
        pltpu.make_async_copy(
            ghost_hbm.at[:, pl.ds(ghost, ghost)], QE.at[:, pl.ds(ghost + planes, ghost)], in_sem.at[2]
        ),
        pltpu.make_async_copy(reg_hbm, REG, in_sem.at[3]),
    ]
    for load in loads:
        load.start()

    barrier = pltpu.get_barrier_semaphore()
    pl.semaphore_signal(barrier, inc=1, device_id={"gx": left}, device_id_type=MESH)
    pl.semaphore_signal(barrier, inc=1, device_id={"gx": right}, device_id_type=MESH)
    for side in y_sides:
        pl.semaphore_signal(barrier, inc=1, device_id={"gy": (up, down)[side]}, device_id_type=MESH)

    sub = lax.broadcasted_iota(jnp.int32, (8, 128), 0)
    lane = lax.broadcasted_iota(jnp.int32, (8, 128), 1)
    low = sub < 4
    lane_group = lax.shift_right_logical(lane, 3)
    lane_first = lax.bitwise_and(lane, 7) < 4

    def x_send(way, r, c, fields):
        return pltpu.make_async_remote_copy(
            src_ref=XS.at[way, r, c, pl.ds(0, fields)],
            dst_ref=XR.at[way, r, c, pl.ds(0, fields)],
            send_sem=xs_sem.at[way, r, c],
            recv_sem=xr_sem.at[way, r, c],
            device_id={"gx": (right, left)[way]},
            device_id_type=MESH,
        )

    def y_send(way, r, c, count):
        return pltpu.make_async_remote_copy(
            src_ref=YS.at[r, c, pl.ds(0, count)],
            dst_ref=YR.at[way, r, c, pl.ds(0, count)],
            send_sem=ys_sem.at[way, r, c],
            recv_sem=yr_sem.at[way, r, c],
            device_id={"gy": (up, down)[way]},
            device_id_type=MESH,
        )

    def xg_send(way):
        return pltpu.make_async_remote_copy(
            src_ref=XSG.at[way],
            dst_ref=XRG.at[way],
            send_sem=gs_sem.at[way],
            recv_sem=gr_sem.at[way],
            device_id={"gx": (right, left)[way]},
            device_id_type=MESH,
        )

    def yg_send(way):
        return pltpu.make_async_remote_copy(
            src_ref=YSG,
            dst_ref=YRG.at[way],
            send_sem=gs_sem.at[2 + way],
            recv_sem=gr_sem.at[2 + way],
            device_id={"gy": (up, down)[way]},
            device_id_type=MESH,
        )

    def exchange(r, c):
        fields, count = ((4, Y_STATE), (5, Y_FLUX))[r % 2]
        return [x_send(way, r, c, fields) for way in (0, 1)] + [y_send(way, r, c, count) for way in y_sides]

    def ghost_exchange():
        return [xg_send(way) for way in (0, 1)] + [yg_send(way) for way in y_sides]

    def pack_high(first, second):
        return jnp.where(low, pltpu.roll(second, 4, 0), first)

    def pack_low(first, second):
        return jnp.where(low, first, pltpu.roll(second, 4, 0))

    def unpack_x(from_left, from_right):
        first = jnp.where(low, from_right, from_left)
        second = pltpu.roll(jnp.where(low, from_left, from_right), 4, 0)
        return first, second

    row = lax.bitwise_and(sub, 3)
    column = lax.bitwise_and(lane, 7)
    edge = jnp.logical_or(lane < 4, lane >= 124)
    low_weights = [jnp.where(row + d <= 3, -stencil[3 - d], 0.0) for d in range(4)]
    high_weights = [jnp.where(row >= d, stencil[3 - d], 0.0) for d in range(4)]

    def inner_x(field):
        a, b, c, _ = stencil
        after = pltpu.roll(field, 7, 0)
        before = pltpu.roll(field, 1, 0)
        middle = b * field
        return pltpu.roll(a * before + middle + c * after, 6, 0) - pltpu.roll(a * after + middle + c * before, 2, 0)

    def inner_y(field):
        a, b, c, d = stencil
        after = pltpu.roll(field, 127, 1)
        before = pltpu.roll(field, 1, 1)
        middle = c * field
        far = pltpu.roll(b * before + middle + d * after, 125, 1) - pltpu.roll(b * after + middle + d * before, 3, 1)
        return a * (after - before) + far

    def edge_x(r, c, f, k):
        gap_low = XR[0, r, c, f, k] - XS[0, r, c, f, k]
        gap_high = XR[1, r, c, f, k] - XS[1, r, c, f, k]
        at_low = low_weights[0] * gap_low
        at_high = high_weights[0] * gap_high
        for d in range(1, 4):
            at_low += low_weights[d] * pltpu.roll(gap_low, 8 - d, 0)
            at_high += high_weights[d] * pltpu.roll(gap_high, d, 0)
        return pltpu.roll(jnp.where(low, at_high, at_low), 4, 0), jnp.where(low, at_low, at_high)

    def edge_y(merged, own):
        gap = merged - own
        total = None
        for o, weight in enumerate(stencil, start=1):
            at_high = jnp.logical_and(column < 4, column + o >= 4)
            at_low = jnp.logical_and(column >= 4, column - o < 4)
            term = jnp.where(at_high, weight, 0.0) * pltpu.roll(gap, 128 - o, 1)
            term += jnp.where(at_low, -weight, 0.0) * pltpu.roll(gap, o, 1)
            total = term if total is None else total + term
        return total

    def place_y(packed, j):
        packed, j = packed[j // 16], j % 16
        return jnp.where(edge, pltpu.roll(packed, (128 - (8 * j + 4)) % 128, 1), 0.0)

    def pack_y(items):
        packed = None
        for j, item in enumerate(items):
            turned = pltpu.roll(item, (8 * j + 4) % 128, 1)
            packed = turned if packed is None else jnp.where(lane_group == j, turned, packed)
        return packed

    def send_y(r, c, items):
        for i in range(0, len(items), 16):
            YS[r, c, i // 16] = pack_y(items[i : i + 16])

    def merge_y(ref, *index):
        if ny == 2:
            return ref[(0,) + index]
        return jnp.where(lane_first, ref[(0,) + index], ref[(1,) + index])

    def unpack_y(merged, j):
        return pltpu.roll(merged, (128 - (8 * j + 4)) % 128, 1)

    def d_x(field, halo):
        total = None
        for s, weight in enumerate(stencil, start=1):
            plus = pltpu.roll(jnp.where(sub < s, halo, field), 8 - s, 0)
            minus = pltpu.roll(jnp.where(sub >= 8 - s, halo, field), s, 0)
            term = weight * (plus - minus)
            total = term if total is None else total + term
        return total

    def d_y(field, halo):
        total = None
        for s, weight in enumerate(stencil, start=1):
            plus = pltpu.roll(jnp.where(lane < s, halo, field), 128 - s, 1)
            minus = pltpu.roll(jnp.where(lane >= 128 - s, halo, field), s, 1)
            term = weight * (plus - minus)
            total = term if total is None else total + term
        return total

    def d_z(ref, f, z):
        total = None
        for s, weight in enumerate(stencil, start=1):
            term = weight * (ref[f, z + s] - ref[f, z - s])
            total = term if total is None else total + term
        return total

    def primitives(q):
        inverse = 1.0 / q[0]
        speeds = [q[1] * inverse, q[2] * inverse, q[3] * inverse]
        kinetic = 0.5 * (q[1] * speeds[0] + q[2] * speeds[1] + q[3] * speeds[2])
        pressure = 0.4 * (q[4] - kinetic)
        return speeds + [1.4 * pressure * inverse, pressure]

    def store_primitives(q, z):
        values = primitives(q)
        for f in range(5):
            PR[f, z] = values[f]
        return values

    def send_state(r, c, values):
        for f in range(4):
            for k in range(HALF):
                XS[0, r, c, f, k] = pack_high(values[k][f], values[k + HALF][f])
                XS[1, r, c, f, k] = pack_low(values[k][f], values[k + HALF][f])
        copies = exchange(r, c)
        for copy in copies[:2]:
            copy.start()
        send_y(r, c, [values[k][f] for f in range(4) for k in range(CH)])
        for copy in copies[2:]:
            copy.start()

    def start_chunk(c, carry):
        values = []
        for k in range(CH):
            z = ghost + c * CH + k
            values.append(store_primitives([QE[f, z] for f in range(5)], z))
        send_state(0, c, values)
        return carry

    def ghost_start():
        near = []
        for z in list(range(ghost)) + list(range(ghost + planes, 2 * ghost + planes)):
            values = store_primitives([QE[f, z] for f in range(5)], z)
            if ghost - 4 <= z < ghost + planes + 4:
                near.append(values)
        for f, field in enumerate((0, 2)):
            for k in range(4):
                XSG[0, f, k] = pack_high(near[k][field], near[k + 4][field])
                XSG[1, f, k] = pack_low(near[k][field], near[k + 4][field])
        YSG[...] = pack_y([near[k][field] for field in (1, 2) for k in range(8)])
        for copy in ghost_exchange():
            copy.start()

    def vertical(z, grads, q, u, p):
        m1, m2, m3, energy = q
        txz, tyz, tzz, heat = grads
        FZ[0, z - 4] = m3
        FZ[1, z - 4] = m1 * u[2] - txz
        FZ[2, z - 4] = m2 * u[2] - tyz
        FZ[3, z - 4] = m3 * u[2] + p - tzz
        FZ[4, z - 4] = (energy + p) * u[2] - (u[0] * txz + u[1] * tyz + u[2] * tzz + heat)

    def gradient_chunk(c, carry):
        for k in range(CH):
            w = c * CH + k
            for f in range(4):
                field = PR[f, ghost + w]
                DX[f, w] = inner_x(field)
                DY[f, w] = inner_y(field)
                DZ[f, w] = d_z(PR, f, ghost + w)
        return carry

    def flux_chunk(r, c, carry):
        for copy in exchange(r, c):
            copy.wait_recv()
        edges = [[None] * CH for _ in range(4)]
        for f in range(4):
            for k in range(HALF):
                edges[f][k], edges[f][k + HALF] = edge_x(r, c, f, k)
        packed = [edge_y(merge_y(YR, r, c, i), YS[r, c, i]) for i in range(Y_STATE)]
        packs_x = []
        packs_y = []
        downs = []
        for k in range(CH):
            z = ghost + c * CH + k
            value = [PR[f, z] for f in range(4)]
            w = c * CH + k
            gx = [DX[f, w] + edges[f][k] for f in range(4)]
            gy = [DY[f, w] + place_y(packed, CH * f + k) for f in range(4)]
            gz = [DZ[f, w] for f in range(4)]
            u = value[:3]
            p = PR[4, z]
            m1, m2, m3, energy = [QE[f, z] for f in range(1, 5)]
            dilation = (2.0 / 3.0 * viscosity) * (gx[0] + gy[1] + gz[2])
            txx = (2.0 * viscosity) * gx[0] - dilation
            tyy = (2.0 * viscosity) * gy[1] - dilation
            tzz = (2.0 * viscosity) * gz[2] - dilation
            txy = viscosity * (gx[1] + gy[0])
            txz = viscosity * (gx[2] + gz[0])
            tyz = viscosity * (gy[2] + gz[1])
            total = energy + p
            flux_x = [
                m1,
                m1 * u[0] + p - txx,
                m2 * u[0] - txy,
                m3 * u[0] - txz,
                total * u[0] - (u[0] * txx + u[1] * txy + u[2] * txz + conductivity * gx[3]),
            ]
            flux_y = [
                m2,
                m1 * u[1] - txy,
                m2 * u[1] + p - tyy,
                m3 * u[1] - tyz,
                total * u[1] - (u[0] * txy + u[1] * tyy + u[2] * tyz + conductivity * gy[3]),
            ]
            packs_x.append(flux_x)
            packs_y.append(flux_y)
            downs.append((z, (txz, tyz, tzz, conductivity * gz[3]), (m1, m2, m3, energy), u, p))
        r = r + 1
        copies = exchange(r, c)
        for f in range(5):
            for k in range(HALF):
                XS[0, r, c, f, k] = pack_high(packs_x[k][f], packs_x[k + HALF][f])
                XS[1, r, c, f, k] = pack_low(packs_x[k][f], packs_x[k + HALF][f])
        for copy in copies[:2]:
            copy.start()
        send_y(r, c, [packs_y[k][f] for f in range(5) for k in range(CH)])
        for copy in copies[2:]:
            copy.start()
        for k in range(CH):
            for f in range(5):
                FX[f, c * CH + k] = packs_x[k][f]
                FY[f, c * CH + k] = packs_y[k][f]
            vertical(*downs[k])
        return carry

    def ghost_gradients():
        for copy in ghost_exchange():
            copy.wait_recv()
        halos = [[None] * 8 for _ in range(2)]
        for f in range(2):
            for k in range(4):
                halos[f][k], halos[f][k + 4] = unpack_x(XRG[0, f, k], XRG[1, f, k])
        merged = merge_y(YRG)
        for k in range(8):
            z = ghost - 4 + k if k < 4 else ghost + planes + k - 4
            u = [PR[f, z] for f in range(3)]
            GH[0, k] = d_x(u[0], halos[0][k]) + d_y(u[1], unpack_y(merged, k))
            GH[1, k] = d_x(u[2], halos[1][k])
            GH[2, k] = d_y(u[2], unpack_y(merged, 8 + k))

    def ghost_flux(k, carry):
        z = ghost - 4 + k + (planes + 4 - 4) * (k // 4)
        gz = [d_z(PR, f, z) for f in range(4)]
        dilation = (2.0 / 3.0 * viscosity) * (GH[0, k] + gz[2])
        tzz = (2.0 * viscosity) * gz[2] - dilation
        txz = viscosity * (GH[1, k] + gz[0])
        tyz = viscosity * (GH[2, k] + gz[1])
        vertical(
            z,
            (txz, tyz, tzz, conductivity * gz[3]),
            [QE[f, z] for f in range(1, 5)],
            [PR[f, z] for f in range(3)],
            PR[4, z],
        )
        return carry

    def slope_chunk(c, carry):
        for k in range(CH):
            w = c * CH + k
            for f in range(5):
                SL[f, w] = inner_x(FX[f, w]) + inner_y(FY[f, w]) + d_z(FZ, f, w + 4)
        return carry

    def update_chunk(section, c, carry):
        r = 2 * section + 1
        for copy in exchange(r, c):
            copy.wait_recv()
        edges = [[None] * CH for _ in range(5)]
        for f in range(5):
            for k in range(HALF):
                edges[f][k], edges[f][k + HALF] = edge_x(r, c, f, k)
        packed = [edge_y(merge_y(YR, r, c, i), YS[r, c, i]) for i in range(Y_FLUX)]
        values = []
        for k in range(CH):
            w = c * CH + k
            z = ghost + w
            q = []
            for f in range(5):
                slope = SL[f, w] + edges[f][k] + place_y(packed, CH * f + k)
                if section == 1:
                    slope_out[f, w] = slope
                    continue
                register = section_a[0] * REG[f, w] - time_step * slope
                register_out[f, w] = register
                state = QE[f, z] + section_b[0] * register
                QE[f, z] = state
                state_out[f, w] = state
                q.append(state)
            if section == 0:
                values.append(store_primitives(q, z))
        if section == 0:
            send_state(2, c, values)
        return carry

    loads[0].wait()
    pl.semaphore_wait(barrier, 2 + len(y_sides))
    lax.fori_loop(0, chunks, start_chunk, 0)
    loads[1].wait()
    loads[2].wait()
    ghost_start()
    for section in range(2):
        lax.fori_loop(0, chunks, gradient_chunk, 0)
        lax.fori_loop(0, chunks, functools.partial(flux_chunk, 2 * section), 0)
        if section == 0:
            ghost_gradients()
            loads[3].wait()
        lax.fori_loop(0, 8, ghost_flux, 0)
        lax.fori_loop(0, chunks, slope_chunk, 0)
        lax.fori_loop(0, chunks, functools.partial(update_chunk, section), 0)

    for copy in ghost_exchange():
        copy.wait_send()

    def finish(c, carry):
        for r in range(4):
            for copy in exchange(r, c):
                copy.wait_send()
        return carry

    lax.fori_loop(0, chunks, finish, 0)


def solution(mesh):
    nx, ny = mesh.shape["gx"], mesh.shape["gy"]

    def body(conserved, register, ghost_planes):
        _, planes, rows, columns = conserved.shape
        assert (rows, columns) == (8, 128) and planes % CH == 0
        chunks = planes // CH
        extended = planes + ghost_planes.shape[1]
        tile = (rows, columns)

        def vmem(*shape):
            return pltpu.VMEM(shape + tile, jnp.float32)

        dma = pltpu.SemaphoreType.DMA
        state, old, slope = pl.pallas_call(
            functools.partial(kernel, nx, ny, chunks),
            out_shape=[pltpu.VMEM(conserved.shape, jnp.float32)] * 3,
            in_specs=[pl.BlockSpec(memory_space=pltpu.HBM)] * 3,
            out_specs=[pl.BlockSpec(memory_space=pltpu.VMEM)] * 3,
            scratch_shapes=[
                vmem(5, extended),
                vmem(5, extended),
                vmem(5, planes),
                vmem(5, planes),
                vmem(5, planes),
                vmem(5, planes + 8),
                vmem(3, 8),
                vmem(4, planes),
                vmem(4, planes),
                vmem(4, planes),
                vmem(5, planes),
                vmem(2, 4, chunks, 5, HALF),
                vmem(2, 4, chunks, 5, HALF),
                vmem(4, chunks, Y_FLUX),
                vmem(2, 4, chunks, Y_FLUX),
                vmem(2, 2, 4),
                vmem(2, 2, 4),
                vmem(),
                vmem(2),
                dma((4,)),
                dma((2, 4, chunks)),
                dma((2, 4, chunks)),
                dma((2, 4, chunks)),
                dma((2, 4, chunks)),
                dma((4,)),
                dma((4,)),
            ],
            compiler_params=pltpu.CompilerParams(
                collective_id=0, has_side_effects=True, vmem_limit_bytes=60 * 1024 * 1024
            ),
        )(conserved, register, ghost_planes)
        carried = section_a[1] * old - time_step * slope
        return state + section_b[1] * carried, carried

    spec = P(None, None, "gx", "gy")
    return jax.shard_map(
        body, mesh=mesh, in_specs=(spec, spec, spec), out_specs=(spec, spec), check_vma=False
    )
```

profile of v0, /device:TPU:0, one launch (start us, length us, event | category | flops | bytes accessed | tf_op | source)
XLA Modules:
  0.0 26.0 jit_solution(9590758512570379184)
XLA Ops:
  0.6 24.4 %shard_map.50 = (f32[5,16,8,128]{3,2,1,0:T(8,128)S(1)}, f32[5,16,8,128]{3,2,1,0:T(8,128)S(1)}, f32[5,16,8,128]{3,2,1,0:T(8,128)S(1)}) custom-call(f32[5,16,8,128]{3,2,1,0:T(8,128)} %cons_hbm.1, f32[5,16,8,128]{3,2,1,0:T(8,128)} %reg_hbm.1, f32[5,16,8,128]{3,2,1,0:T(8,128)} %ghost_hbm.1), custom_call_target="tpu_custom_call" | custom-call | tf_op jit(solution)/shard_map/pallas_call | solution.py:483
  25.1 0.9 %multiply_add_fusion = (f32[5,16,8,128]{3,2,1,0:T(8,128)}, f32[5,16,8,128]{3,2,1,0:T(8,128)}) fusion(f32[5,16,8,128]{3,2,1,0:T(8,128)S(1)} %get-tuple-element.5, f32[5,16,8,128]{3,2,1,0:T(8,128)S(1)} %get-tuple-element.7, f32[5,16,8,128]{3,2,1,0:T(8,128)S(1)} %get-tuple-element.6), kind=kLoop, calls=%fused_computation | loop fusion | flops 409600 | bytes 1638400 | tf_op jit(solution)/shard_map/add | solution.py:521
where the time goes:
time: 26.1 us; the launch traced here: 26 us
  Pallas kernels  24.4 us (93%)
  other arithmetic  0.91 us (3%)
  between operations  0.64 us (2%)
    pallas_call x1, Pallas kernels, body(): pl.pallas_call(functools.partial(kernel, nx, ny, chunks), out_shape=[pltp...  24.4 us
    add x1, other arithmetic, body(): return (state + section_b[1] * carried, carried)  0.91 us

commit v1 on v0

v1 whole, which is shorter than its diff:
```python
import functools

import jax
import jax.numpy as jnp
from jax import lax
from jax.experimental import pallas as pl
from jax.experimental.pallas import tpu as pltpu
from jax.sharding import PartitionSpec as P
import numpy as np

MESH = pl.DeviceIdType.MESH

viscosity = 0.15
conductivity = 0.15 / (0.4 * 0.7)
time_step = 0.2
section_a = (-0.41789047, -1.19215169)
section_b = (0.37921031, 0.82295503)
stencil = (0.8, -0.2, 4.0 / 105.0, -1.0 / 280.0)
coarse = [float(np.asarray(w, jnp.bfloat16)) for w in stencil]
fine = [w - c for w, c in zip(stencil, coarse, strict=True)]
CH = 4
HALF = CH // 2
GHOST = 8
SENT = HALF + 4 * CH
SLOTS = SENT + HALF
OWN = pl.ds(8, 8)
BEFORE = pl.ds(0, 8)
AFTER = pl.ds(16, 8)


def kernel(
    nx,
    ny,
    chunks,
    cons_hbm,
    reg_hbm,
    ghost_hbm,
    state_out,
    register_out,
    slope_out,
    QE,
    REG,
    XE,
    YP,
    YN,
    CP,
    CN,
    HH,
    XSG,
    XRG,
    DY,
    DZ,
    FX,
    FY,
    FZ,
    RS,
    GH,
    SD,
    ED,
    HE,
    HD,
    W,
    in_sem,
    xs_sem,
    xr_sem,
    ys_sem,
    yr_sem,
    ds_sem,
    dr_sem,
    gs_sem,
    gr_sem,
):
    ix = lax.axis_index("gx")
    iy = lax.axis_index("gy")
    beside = (lax.rem(ix + 1, nx), lax.rem(ix + nx - 1, nx))
    across = (lax.rem(iy + 1, ny), lax.rem(iy + ny - 1, ny))
    y_sides = (0,) if ny == 2 else (0, 1)

    planes = chunks * CH
    loads = [
        pltpu.make_async_copy(cons_hbm, QE.at[:, pl.ds(GHOST, planes)], in_sem.at[0]),
        pltpu.make_async_copy(ghost_hbm.at[:, pl.ds(0, GHOST)], QE.at[:, pl.ds(0, GHOST)], in_sem.at[1]),
        pltpu.make_async_copy(
            ghost_hbm.at[:, pl.ds(GHOST, GHOST)], QE.at[:, pl.ds(GHOST + planes, GHOST)], in_sem.at[2]
        ),
        pltpu.make_async_copy(reg_hbm, REG, in_sem.at[3]),
    ]
    for load in loads:
        load.start()

    barrier = pltpu.get_barrier_semaphore()
    neighbours = [{"gx": x} for x in beside]
    neighbours += [{"gy": across[way]} for way in y_sides]
    neighbours += [{"gx": x, "gy": across[way]} for x in beside for way in y_sides]
    for neighbour in neighbours:
        pl.semaphore_signal(barrier, inc=1, device_id=neighbour, device_id_type=MESH)

    sub = lax.broadcasted_iota(jnp.int32, (8, 128), 0)
    lane = lax.broadcasted_iota(jnp.int32, (8, 128), 1)
    low = sub < 4
    edge = jnp.logical_or(lane < 4, lane >= 124)
    first_half = lane < 64
    lane_half = lax.bitwise_and(lane, 63)
    lane_group = lax.shift_right_logical(lane_half, 4)
    late = lax.bitwise_and(lane, 15) >= 8
    own_lane = jnp.logical_xor(late, lane >= 64)

    def x_copy(way, s, c):
        slots = pl.ds((0, HALF)[way], SENT)
        return pltpu.make_async_remote_copy(
            src_ref=XE.at[s, c + 2, slots, OWN],
            dst_ref=XE.at[s, c + 2, slots, (BEFORE, AFTER)[way]],
            send_sem=xs_sem.at[way, s, c],
            recv_sem=xr_sem.at[way, s, c],
            device_id={"gx": beside[way]},
            device_id_type=MESH,
        )

    def y_copy(way, s, c):
        return pltpu.make_async_remote_copy(
            src_ref=YP.at[s, c + 1],
            dst_ref=YN.at[way, s, c + 1],
            send_sem=ys_sem.at[way, s, c],
            recv_sem=yr_sem.at[way, s, c],
            device_id={"gy": across[way]},
            device_id_type=MESH,
        )

    def d_copy(x_way, way, s, c):
        return pltpu.make_async_remote_copy(
            src_ref=CP.at[x_way, s, c],
            dst_ref=CN.at[way, x_way, s, c],
            send_sem=ds_sem.at[x_way, way, s, c],
            recv_sem=dr_sem.at[x_way, way, s, c],
            device_id={"gx": beside[x_way], "gy": across[way]},
            device_id_type=MESH,
        )

    def exchange(s, c):
        copies = [x_copy(way, s, c) for way in (0, 1)]
        copies += [d_copy(x_way, way, s, c) for x_way in (0, 1) for way in y_sides]
        return copies + [y_copy(way, s, c) for way in y_sides]

    def ghost_exchange():
        copies = []
        for way in (0, 1):
            copies.append(
                pltpu.make_async_remote_copy(
                    src_ref=XSG.at[way],
                    dst_ref=XRG.at[way],
                    send_sem=gs_sem.at[way],
                    recv_sem=gr_sem.at[way],
                    device_id={"gx": beside[way]},
                    device_id_type=MESH,
                )
            )
        for way in y_sides:
            for i, e in enumerate((0, chunks + 1)):
                copies.append(
                    pltpu.make_async_remote_copy(
                        src_ref=YP.at[0, e, pl.ds(1, 2)],
                        dst_ref=YN.at[way, 0, e, pl.ds(1, 2)],
                        send_sem=gs_sem.at[2 + 2 * way + i],
                        recv_sem=gr_sem.at[2 + 2 * way + i],
                        device_id={"gy": across[way]},
                        device_id_type=MESH,
                    )
                )
        return copies

    def pack_high(first, second):
        return jnp.where(low, pltpu.roll(second, 4, 0), first)

    def pack_low(first, second):
        return jnp.where(low, first, pltpu.roll(second, 4, 0))

    def unpack_x(from_left, from_right):
        first = jnp.where(low, from_right, from_left)
        second = pltpu.roll(jnp.where(low, from_left, from_right), 4, 0)
        return first, second

    def pack_y(items):
        packed = None
        for k, item in enumerate(items):
            turned = jnp.where(first_half, pltpu.roll(item, 16 * k + 8, 1), pltpu.roll(item, 16 * k + 72, 1))
            packed = turned if packed is None else jnp.where(lane_group == k, turned, packed)
        return packed

    def by_side(values):
        return values[0] if ny == 2 else jnp.where(first_half, values[0], values[1])

    def both_edges(strip):
        return jnp.where(late, strip, pltpu.roll(strip, 64, 1))

    def place(edges, k, inner):
        return jnp.where(edge, pltpu.roll(edges, 128 - (16 * k + 8), 1), inner)

    def add(edges, k, inner):
        return inner + jnp.where(edge, pltpu.roll(edges, 128 - (16 * k + 8), 1), 0.0)

    def weighted(pairs):
        total = None
        for weight, (plus, minus) in zip(stencil, pairs, strict=True):
            term = weight * (plus - minus)
            total = term if total is None else total + term
        return total

    def band(items):
        flat = jnp.concatenate(items, axis=0) if isinstance(items, list) else items.reshape(-1, 128)
        high = flat.astype(jnp.bfloat16)
        rest = (flat - high.astype(jnp.float32)).astype(jnp.bfloat16)
        out = jnp.dot(jnp.concatenate([high, rest], axis=1), W[...], preferred_element_type=jnp.float32)
        return (out[:, :128] + out[:, 128:]).reshape(-1, 8, 128)

    def d_rows(ref, index, start):
        return weighted(
            [(ref[index + (pl.ds(start + s, 8),)], ref[index + (pl.ds(start - s, 8),)]) for s in range(1, 5)]
        )

    def d_x(field, halo):
        return weighted(
            [
                (
                    pltpu.roll(jnp.where(sub < s, halo, field), 8 - s, 0),
                    pltpu.roll(jnp.where(sub >= 8 - s, halo, field), s, 0),
                )
                for s in range(1, 5)
            ]
        )

    def d_z(ref, f, z):
        return weighted([(ref[f, z + s], ref[f, z - s]) for s in range(1, 5)])

    def tile(s, c, f, k):
        return XE[s, c + k // CH, HALF + CH * f + k % CH, OWN]

    def d_z_tile(s, c, f, k):
        return weighted([(tile(s, c, f, k + o), tile(s, c, f, k - o)) for o in range(1, 5)])

    def d_z_strip(s, c, f):
        values = []
        for way in y_sides:
            before, here, after = [YN[way, s, c + i, f] for i in range(3)]
            pairs = [
                (
                    pltpu.roll(jnp.where(lane_half < 16 * o, after, here), 128 - 16 * o, 1),
                    pltpu.roll(jnp.where(lane_half >= 64 - 16 * o, before, here), 16 * o, 1),
                )
                for o in range(1, 4)
            ]
            values.append(weighted(pairs + [(after, before)]))
        return by_side(values)

    def primitives(q):
        inverse = 1.0 / q[0]
        speeds = [q[1] * inverse, q[2] * inverse, q[3] * inverse]
        kinetic = 0.5 * (q[1] * speeds[0] + q[2] * speeds[1] + q[3] * speeds[2])
        pressure = 0.4 * (q[4] - kinetic)
        return speeds + [1.4 * pressure * inverse]

    def thermal(rho, v):
        m = [rho * v[i] for i in range(3)]
        p = (1.0 / 1.4) * (rho * v[3])
        total = 3.5 * p + 0.5 * (m[0] * v[0] + m[1] * v[1] + m[2] * v[2])
        return m, p, total

    def flux(along, v, state, stress, gradient):
        m, p, total = state
        out = [m[along]]
        for i in range(3):
            entry = m[i] * v[along] - stress[i]
            out.append(entry + p if i == along else entry)
        work = v[0] * stress[0] + v[1] * stress[1] + v[2] * stress[2] + conductivity * gradient
        out.append(total * v[along] - work)
        return out

    def shrink(gx, gy, gz):
        return (2.0 / 3.0 * viscosity) * (gx + gy + gz)

    def put(s, c, values):
        for f in range(4):
            for k in range(CH):
                XE[s, c, HALF + CH * f + k, OWN] = values[k][f]

    def prepare(s, c, values, rho):
        put(s, c + 2, values)
        for j in range(HALF):
            XE[s, c + 2, j, OWN] = pack_high(rho[j], rho[j + HALF])
            XE[s, c + 2, SENT + j, OWN] = pack_low(rho[j], rho[j + HALF])
        packs = [pack_y([values[k][f] for k in range(CH)]) for f in range(4)] + [pack_y(rho)]
        for f in range(5):
            YP[s, c + 1, f] = packs[f]
        CP[0, s, c] = pack_high(packs[0], packs[1])
        CP[1, s, c] = pack_low(packs[0], packs[1])

    def start_chunk(c, carry):
        states = [[QE[f, GHOST + c * CH + k] for f in range(5)] for k in range(CH)]
        prepare(0, c, [primitives(q) for q in states], [q[0] for q in states])
        return carry

    def send_chunk(c, carry):
        for copy in exchange(0, c):
            copy.start()
        return carry

    def ghost_start():
        near = []
        for c in (0, 1, chunks + 2, chunks + 3):
            values = [primitives([QE[f, c * CH + k] for f in range(5)]) for k in range(CH)]
            for s in range(2):
                put(s, c, values)
            if c in (1, chunks + 2):
                near += values
                e = 0 if c == 1 else chunks + 1
                for f in (1, 2):
                    YP[0, e, f] = pack_y([values[k][f] for k in range(CH)])
        for i, f in enumerate((0, 2)):
            for k in range(4):
                XSG[0, i, k] = pack_high(near[k][f], near[k + 4][f])
                XSG[1, i, k] = pack_low(near[k][f], near[k + 4][f])

    def gradients_y(s):
        DY[...] = band(XE[s, pl.ds(2, chunks), pl.ds(HALF, 4 * CH), OWN]).reshape(DY.shape)

    def gradient_chunk(s, c, carry):
        for k in range(CH):
            for f in range(4):
                DZ[f, c * CH + k] = d_z_tile(s, c + 2, f, k)
        return carry

    def ghost_gradients():
        for copy in ghost_exchange():
            copy.wait_recv()
        sides = ((0, 0, 1), (chunks + 1, planes + 4, chunks + 2))
        items = []
        for e, _, c in sides:
            for f in (1, 2):
                for way in y_sides:
                    YN[way, 1, e, f] = YN[way, 0, e, f]
                merged = by_side([YN[way, 0, e, f] for way in y_sides])
                items.append(jnp.where(own_lane, YP[0, e, f], merged))
        for _, _, c in sides:
            items += [tile(0, c, f, k) for f in (1, 2) for k in range(CH)]
        out = band(items)
        for i, (_, at, c) in enumerate(sides):
            strips = [both_edges(out[2 * i + f]) for f in range(2)]
            inner = 4 + 2 * CH * i
            for k in range(CH):
                j = CH * i + k
                halos = []
                for n, f in enumerate((0, 2)):
                    halo = unpack_x(XRG[0, n, k], XRG[1, n, k])[i]
                    HH[f, at + k] = halo
                    halos.append(halo)
                GH[0, j] = d_x(tile(0, c, 0, k), halos[0]) + place(strips[0], k, out[inner + k])
                GH[1, j] = d_x(tile(0, c, 2, k), halos[1])
                GH[2, j] = place(strips[1], k, out[inner + CH + k])

    def ghost_flux(s):
        for e, at, c in ((0, 0, 1), (1, planes + 4, chunks + 2)):
            for k in range(CH):
                j = CH * e + k
                v = [tile(s, c, f, k) for f in range(4)]
                gz = [d_z_tile(s, c, f, k) for f in range(4)]
                dilation = (2.0 / 3.0 * viscosity) * (GH[0, j] + gz[2])
                stress = [
                    viscosity * (GH[1, j] + gz[0]),
                    viscosity * (GH[2, j] + gz[1]),
                    (2.0 * viscosity) * gz[2] - dilation,
                ]
                out = flux(2, v, thermal(QE[0, c * CH + k], v), stress, gz[3])
                for f in range(5):
                    FZ[f, at + k] = out[f]

    def beyond(s, c, f):
        return by_side([YN[way, s, c + 1, f] for way in y_sides])

    def corners(s, c):
        pairs = [unpack_x(CN[way, 0, s, c], CN[way, 1, s, c]) for way in y_sides]
        return [by_side([pair[f] for pair in pairs]) for f in range(2)]

    def arrive(s, c):
        for copy in exchange(s, c):
            copy.wait_recv()
        items = [jnp.where(own_lane, YP[s, c + 1, f], beyond(s, c, f)) for f in range(4)]
        items += [jnp.where(own_lane, 0.0, corner) for corner in corners(s, c)]
        for f in range(4):
            for k in range(CH):
                slot = HALF + CH * f + k
                halo = jnp.where(low, XE[s, c + 2, slot, AFTER], XE[s, c + 2, slot, BEFORE])
                HH[f, 4 + c * CH + k] = halo
                if f < 2:
                    items.append(halo)
        out = band(items)
        for f in range(4):
            SD[f, c] = out[f]
            ED[f, c] = both_edges(out[f])
        for f in range(2):
            HE[f, c] = both_edges(out[4 + f])
            for k in range(CH):
                HD[f, c * CH + k] = out[6 + CH * f + k]

    def strip_chunk(s, c):
        v = [beyond(s, c, f) for f in range(5)]
        strip_x = [d_x(v[f], corner) for f, corner in enumerate(corners(s, c))]
        strip_y = [SD[f, c] for f in range(4)]
        strip_z = [d_z_strip(s, c, f) for f in (1, 2)]
        dilation = shrink(strip_x[0], strip_y[1], strip_z[1])
        stress = [
            viscosity * (strip_x[1] + strip_y[0]),
            (2.0 * viscosity) * strip_y[1] - dilation,
            viscosity * (strip_y[2] + strip_z[0]),
        ]
        out = flux(1, v, thermal(v[4], v), stress, strip_y[3])
        out = band([jnp.where(own_lane, 0.0, out[min(f, 4)]) for f in range(6)])
        for f in range(5):
            RS[f, c] = both_edges(out[f])

    def flux_chunk(s, c):
        halo_rho = [None] * CH
        for j in range(HALF):
            halo_rho[j], halo_rho[j + HALF] = unpack_x(XE[s, c + 2, j, BEFORE], XE[s, c + 2, SENT + j, AFTER])
        for k in range(CH):
            w = c * CH + k
            gx = []
            halo_gx = []
            for f in range(4):
                index = (s, c + 2, HALF + CH * f + k)
                lower = d_rows(XE, index, 4)
                upper = d_rows(XE, index, 12)
                gx.append(pltpu.roll(jnp.where(low, upper, lower), 4, 0))
                halo_gx.append(pltpu.roll(jnp.where(low, lower, upper), 4, 0))

            v = [HH[f, 4 + w] for f in range(4)]
            gy = [add(HE[f, c], k, HD[f, w]) for f in range(2)]
            gz = [d_z(HH, f, 4 + w) for f in (0, 2)]
            dilation = shrink(halo_gx[0], gy[1], gz[1])
            stress = [
                (2.0 * viscosity) * halo_gx[0] - dilation,
                viscosity * (halo_gx[1] + gy[0]),
                viscosity * (halo_gx[2] + gz[0]),
            ]
            out = flux(0, v, thermal(halo_rho[k], v), stress, halo_gx[3])
            for f in range(5):
                FX[f, w, BEFORE] = out[f]
                FX[f, w, AFTER] = out[f]

            v = [tile(s, c + 2, f, k) for f in range(4)]
            state = thermal(QE[0, GHOST + w], v)
            gy = [place(ED[f, c], k, DY[c, CH * f + k]) for f in range(4)]
            gz = [DZ[f, w] for f in range(4)]
            dilation = shrink(gx[0], gy[1], gz[2])
            txx = (2.0 * viscosity) * gx[0] - dilation
            tyy = (2.0 * viscosity) * gy[1] - dilation
            tzz = (2.0 * viscosity) * gz[2] - dilation
            txy = viscosity * (gx[1] + gy[0])
            txz = viscosity * (gx[2] + gz[0])
            tyz = viscosity * (gy[2] + gz[1])
            out_x = flux(0, v, state, [txx, txy, txz], gx[3])
            out_y = flux(1, v, state, [txy, tyy, tyz], gy[3])
            out_z = flux(2, v, state, [txz, tyz, tzz], gz[3])
            for f in range(5):
                FX[f, w, OWN] = out_x[f]
                FY[c, CH * f + k] = out_y[f]
                FZ[f, w + 4] = out_z[f]

    def update_chunk(s, c):
        inner = band(FY[c])
        values = []
        rho = []
        for k in range(CH):
            w = c * CH + k
            z = GHOST + w
            q = []
            for f in range(5):
                slope = d_rows(FX, (f, w), 8) + add(RS[f, c], k, inner[CH * f + k]) + d_z(FZ, f, w + 4)
                if s == 1:
                    slope_out[f, w] = slope
                    continue
                register = section_a[0] * REG[f, w] - time_step * slope
                register_out[f, w] = register
                state = QE[f, z] + section_b[0] * register
                QE[f, z] = state
                state_out[f, w] = state
                q.append(state)
            if s == 0:
                values.append(primitives(q))
                rho.append(q[0])
        if s == 0:
            prepare(1, c, values, rho)
            for copy in exchange(1, c):
                copy.start()

    def step(s, c, carry):
        @pl.when(c + 2 < chunks)
        def _():
            arrive(s, c + 2)

        @pl.when(c + 1 < chunks)
        def _():
            strip_chunk(s, c + 1)
            flux_chunk(s, c + 1)

        @pl.when(c >= 0)
        def _():
            update_chunk(s, c)

        return carry

    offset = lax.broadcasted_iota(jnp.int32, (128, 128), 0) - lax.broadcasted_iota(jnp.int32, (128, 128), 1)
    distance = jnp.abs(offset)
    for weights, part in ((coarse, pl.ds(0, 128)), (fine, pl.ds(128, 128))):
        taps = jnp.zeros((128, 128), jnp.float32)
        for o, weight in enumerate(weights, start=1):
            taps = jnp.where(distance == o, weight, taps)
        taps = jnp.where(offset < 0, -taps, taps).astype(jnp.bfloat16)
        W[pl.ds(0, 128), part] = taps
        W[pl.ds(128, 128), part] = taps

    loads[0].wait()
    lax.fori_loop(0, chunks, start_chunk, 0)
    loads[1].wait()
    loads[2].wait()
    ghost_start()
    pl.semaphore_wait(barrier, len(neighbours))
    for copy in ghost_exchange():
        copy.start()
    lax.fori_loop(0, chunks, send_chunk, 0)
    for s in range(2):
        gradients_y(s)
        lax.fori_loop(0, chunks, functools.partial(gradient_chunk, s), 0)
        if s == 0:
            ghost_gradients()
            loads[3].wait()
        ghost_flux(s)
        arrive(s, 0)
        lax.fori_loop(-1, chunks, functools.partial(step, s), 0)

    for copy in ghost_exchange():
        copy.wait_send()

    def finish(c, carry):
        for s in range(2):
            for copy in exchange(s, c):
                copy.wait_send()
        return carry

    lax.fori_loop(0, chunks, finish, 0)


def solution(mesh):
    nx, ny = mesh.shape["gx"], mesh.shape["gy"]
    sides = 1 if ny == 2 else 2

    def body(conserved, register, ghost_planes):
        _, planes, rows, columns = conserved.shape
        assert (rows, columns) == (8, 128) and planes % CH == 0 and ghost_planes.shape[1] == 2 * GHOST
        chunks = planes // CH

        def vmem(*shape, rows=8):
            return pltpu.VMEM(shape + (rows, columns), jnp.float32)

        dma = pltpu.SemaphoreType.DMA
        state, old, slope = pl.pallas_call(
            functools.partial(kernel, nx, ny, chunks),
            out_shape=[pltpu.VMEM(conserved.shape, jnp.float32)] * 3,
            in_specs=[pl.BlockSpec(memory_space=pltpu.HBM)] * 3,
            out_specs=[pl.BlockSpec(memory_space=pltpu.VMEM)] * 3,
            scratch_shapes=[
                vmem(5, planes + 2 * GHOST),
                vmem(5, planes),
                vmem(2, chunks + 4, SLOTS, rows=24),
                vmem(2, chunks + 2, 5),
                vmem(sides, 2, chunks + 2, 5),
                vmem(2, 2, chunks),
                vmem(sides, 2, 2, chunks),
                vmem(4, planes + 8),
                vmem(2, 2, 4),
                vmem(2, 2, 4),
                vmem(chunks, 4 * CH),
                vmem(4, planes),
                vmem(5, planes, rows=24),
                vmem(chunks, 5 * CH),
                vmem(5, planes + 8),
                vmem(5, chunks),
                vmem(3, 8),
                vmem(4, chunks),
                vmem(4, chunks),
                vmem(2, chunks),
                vmem(2, planes),
                pltpu.VMEM((256, 256), jnp.bfloat16),
                dma((4,)),
                dma((2, 2, chunks)),
                dma((2, 2, chunks)),
                dma((sides, 2, chunks)),
                dma((sides, 2, chunks)),
                dma((2, sides, 2, chunks)),
                dma((2, sides, 2, chunks)),
                dma((2 + 2 * sides,)),
                dma((2 + 2 * sides,)),
            ],
            compiler_params=pltpu.CompilerParams(
                collective_id=0, has_side_effects=True, vmem_limit_bytes=60 * 1024 * 1024
            ),
        )(conserved, register, ghost_planes)
        carried = section_a[1] * old - time_step * slope
        return state + section_b[1] * carried, carried

    spec = P(None, None, "gx", "gy")
    return jax.shard_map(
        body, mesh=mesh, in_specs=(spec, spec, spec), out_specs=(spec, spec), check_vma=False
    )
```

time: 26.1 us -> 25.9 us (level)
  the two profiles are of different devices: /device:TPU:0 before, /device:TPU:1 now
where the time goes in v1:
time: 25.9 us; the launch traced here: 25.7 us
  Pallas kernels  24.2 us (93%)
  other arithmetic  0.91 us (4%)
  between operations  0.64 us (2%)
    pallas_call x1, Pallas kernels, body(): pl.pallas_call(functools.partial(kernel, nx, ny, chunks), out_shape=[pltp...  24.2 us
    add x1, other arithmetic, body(): return (state + section_b[1] * carried, carried)  0.91 us

profile of v1, /device:TPU:1, one launch (start us, length us, event | category | flops | bytes accessed | tf_op | source)
XLA Modules:
  0.0 25.7 jit_solution(15467844324223825906)
XLA Ops:
  0.6 24.2 %shard_map.50 = (f32[5,16,8,128]{3,2,1,0:T(8,128)S(1)}, f32[5,16,8,128]{3,2,1,0:T(8,128)S(1)}, f32[5,16,8,128]{3,2,1,0:T(8,128)S(1)}) custom-call(f32[5,16,8,128]{3,2,1,0:T(8,128)} %cons_hbm.1, f32[5,16,8,128]{3,2,1,0:T(8,128)} %reg_hbm.1, f32[5,16,8,128]{3,2,1,0:T(8,128)} %ghost_hbm.1), custom_call_target="tpu_custom_call" | custom-call | tf_op jit(solution)/shard_map/pallas_call | solution.py:564
  24.8 0.9 %multiply_add_fusion = (f32[5,16,8,128]{3,2,1,0:T(8,128)}, f32[5,16,8,128]{3,2,1,0:T(8,128)}) fusion(f32[5,16,8,128]{3,2,1,0:T(8,128)S(1)} %get-tuple-element.5, f32[5,16,8,128]{3,2,1,0:T(8,128)S(1)} %get-tuple-element.7, f32[5,16,8,128]{3,2,1,0:T(8,128)S(1)} %get-tuple-element.6), kind=kLoop, calls=%fused_computation | loop fusion | flops 409600 | bytes 1638400 | tf_op jit(solution)/shard_map/add | solution.py:607

commit v2 on v1

--- a/solution.py
+++ b/solution.py
@@ -59,6 +59,7 @@
     ED,
     HE,
     HD,
+    HX,
     W,
     in_sem,
     xs_sem,
@@ -416,35 +417,37 @@
         for f in range(5):
             RS[f, c] = both_edges(out[f])
 
+    def halo_chunk(s, c):
+        rho = [None] * CH
+        for j in range(HALF):
+            rho[j], rho[j + HALF] = unpack_x(XE[s, c + 2, j, BEFORE], XE[s, c + 2, SENT + j, AFTER])
+        for k in range(CH):
+            w = c * CH + k
+            v = [HH[f, 4 + w] for f in range(4)]
+            gx = [HX[f, w] for f in range(4)]
+            gy = [add(HE[f, c], k, HD[f, w]) for f in range(2)]
+            gz = [d_z(HH, f, 4 + w) for f in (0, 2)]
+            dilation = shrink(gx[0], gy[1], gz[1])
+            stress = [
+                (2.0 * viscosity) * gx[0] - dilation,
+                viscosity * (gx[1] + gy[0]),
+                viscosity * (gx[2] + gz[0]),
+            ]
+            out = flux(0, v, thermal(rho[k], v), stress, gx[3])
+            for f in range(5):
+                FX[f, w, BEFORE] = out[f]
+                FX[f, w, AFTER] = out[f]
+
     def flux_chunk(s, c):
-        halo_rho = [None] * CH
-        for j in range(HALF):
-            halo_rho[j], halo_rho[j + HALF] = unpack_x(XE[s, c + 2, j, BEFORE], XE[s, c + 2, SENT + j, AFTER])
         for k in range(CH):
             w = c * CH + k
             gx = []
-            halo_gx = []
             for f in range(4):
                 index = (s, c + 2, HALF + CH * f + k)
                 lower = d_rows(XE, index, 4)
                 upper = d_rows(XE, index, 12)
                 gx.append(pltpu.roll(jnp.where(low, upper, lower), 4, 0))
-                halo_gx.append(pltpu.roll(jnp.where(low, lower, upper), 4, 0))
-
-            v = [HH[f, 4 + w] for f in range(4)]
-            gy = [add(HE[f, c], k, HD[f, w]) for f in range(2)]
-            gz = [d_z(HH, f, 4 + w) for f in (0, 2)]
-            dilation = shrink(halo_gx[0], gy[1], gz[1])
-            stress = [
-                (2.0 * viscosity) * halo_gx[0] - dilation,
-                viscosity * (halo_gx[1] + gy[0]),
-                viscosity * (halo_gx[2] + gz[0]),
-            ]
-            out = flux(0, v, thermal(halo_rho[k], v), stress, halo_gx[3])
-            for f in range(5):
-                FX[f, w, BEFORE] = out[f]
-                FX[f, w, AFTER] = out[f]
-
+                HX[f, w] = pltpu.roll(jnp.where(low, lower, upper), 4, 0)
             v = [tile(s, c + 2, f, k) for f in range(4)]
             state = thermal(QE[0, GHOST + w], v)
             gy = [place(ED[f, c], k, DY[c, CH * f + k]) for f in range(4)]
@@ -491,21 +494,14 @@
             for copy in exchange(1, c):
                 copy.start()
 
-    def step(s, c, carry):
-        @pl.when(c + 2 < chunks)
-        def _():
-            arrive(s, c + 2)
-
-        @pl.when(c + 1 < chunks)
-        def _():
-            strip_chunk(s, c + 1)
+    def step(s, c):
+        if c + 1 < chunks:
+            arrive(s, c + 1)
             flux_chunk(s, c + 1)
-
-        @pl.when(c >= 0)
-        def _():
+        if c >= 0:
+            strip_chunk(s, c)
+            halo_chunk(s, c)
             update_chunk(s, c)
-
-        return carry
 
     offset = lax.broadcasted_iota(jnp.int32, (128, 128), 0) - lax.broadcasted_iota(jnp.int32, (128, 128), 1)
     distance = jnp.abs(offset)
@@ -518,7 +514,8 @@
         W[pl.ds(128, 128), part] = taps
 
     loads[0].wait()
-    lax.fori_loop(0, chunks, start_chunk, 0)
+    for c in range(chunks):
+        start_chunk(c, 0)
     loads[1].wait()
     loads[2].wait()
     ghost_start()
@@ -528,13 +525,14 @@
     lax.fori_loop(0, chunks, send_chunk, 0)
     for s in range(2):
         gradients_y(s)
-        lax.fori_loop(0, chunks, functools.partial(gradient_chunk, s), 0)
+        for c in range(chunks):
+            gradient_chunk(s, c, 0)
         if s == 0:
             ghost_gradients()
             loads[3].wait()
         ghost_flux(s)
-        arrive(s, 0)
-        lax.fori_loop(-1, chunks, functools.partial(step, s), 0)
+        for c in range(-1, chunks):
+            step(s, c)
 
     for copy in ghost_exchange():
         copy.wait_send()
@@ -588,6 +586,7 @@
                 vmem(4, chunks),
                 vmem(2, chunks),
                 vmem(2, planes),
+                vmem(4, planes),
                 pltpu.VMEM((256, 256), jnp.bfloat16),
                 dma((4,)),
                 dma((2, 2, chunks)),

time: 25.9 us -> 24 us (0.927)
  Pallas kernels: 24.2 us -> 22.3 us
    pallas_call x1, Pallas kernels: 24.2 us -> 22.3 us  [body(): pl.pallas_call(functools.partial(kernel, nx, ny, chunks), out_shape=[pltp...]
where the time goes in v2:
time: 24 us; the launch traced here: 23.9 us
  Pallas kernels  22.3 us (93%)
  other arithmetic  0.91 us (4%)
  between operations  0.64 us (3%)
    pallas_call x1, Pallas kernels, body(): pl.pallas_call(functools.partial(kernel, nx, ny, chunks), out_shape=[pltp...  22.3 us
    add x1, other arithmetic, body(): return (state + section_b[1] * carried, carried)  0.91 us

profile of v2, /device:TPU:1, one launch (start us, length us, event | category | flops | bytes accessed | tf_op | source)
XLA Modules:
  0.0 23.9 jit_solution(175489252608007450)
XLA Ops:
  0.6 22.3 %shard_map.50 = (f32[5,16,8,128]{3,2,1,0:T(8,128)S(1)}, f32[5,16,8,128]{3,2,1,0:T(8,128)S(1)}, f32[5,16,8,128]{3,2,1,0:T(8,128)S(1)}) custom-call(f32[5,16,8,128]{3,2,1,0:T(8,128)} %cons_hbm.1, f32[5,16,8,128]{3,2,1,0:T(8,128)} %reg_hbm.1, f32[5,16,8,128]{3,2,1,0:T(8,128)} %ghost_hbm.1), custom_call_target="tpu_custom_call" | custom-call | tf_op jit(solution)/shard_map/pallas_call | solution.py:562
  23.0 0.9 %multiply_add_fusion = (f32[5,16,8,128]{3,2,1,0:T(8,128)}, f32[5,16,8,128]{3,2,1,0:T(8,128)}) fusion(f32[5,16,8,128]{3,2,1,0:T(8,128)S(1)} %get-tuple-element.5, f32[5,16,8,128]{3,2,1,0:T(8,128)S(1)} %get-tuple-element.7, f32[5,16,8,128]{3,2,1,0:T(8,128)S(1)} %get-tuple-element.6), kind=kLoop, calls=%fused_computation | loop fusion | flops 409600 | bytes 1638400 | tf_op jit(solution)/shard_map/add | solution.py:606

commit v3 on v2

--- a/solution.py
+++ b/solution.py
@@ -79,11 +79,11 @@
 
     planes = chunks * CH
     loads = [
-        pltpu.make_async_copy(cons_hbm, QE.at[:, pl.ds(GHOST, planes)], in_sem.at[0]),
         pltpu.make_async_copy(ghost_hbm.at[:, pl.ds(0, GHOST)], QE.at[:, pl.ds(0, GHOST)], in_sem.at[1]),
         pltpu.make_async_copy(
             ghost_hbm.at[:, pl.ds(GHOST, GHOST)], QE.at[:, pl.ds(GHOST + planes, GHOST)], in_sem.at[2]
         ),
+        pltpu.make_async_copy(cons_hbm, QE.at[:, pl.ds(GHOST, planes)], in_sem.at[0]),
         pltpu.make_async_copy(reg_hbm, REG, in_sem.at[3]),
     ]
     for load in loads:
@@ -138,9 +138,9 @@
         )
 
     def exchange(s, c):
-        copies = [x_copy(way, s, c) for way in (0, 1)]
-        copies += [d_copy(x_way, way, s, c) for x_way in (0, 1) for way in y_sides]
-        return copies + [y_copy(way, s, c) for way in y_sides]
+        copies = [d_copy(x_way, way, s, c) for x_way in (0, 1) for way in y_sides]
+        copies += [y_copy(way, s, c) for way in y_sides]
+        return copies + [x_copy(way, s, c) for way in (0, 1)]
 
     def ghost_exchange():
         copies = []
@@ -291,8 +291,9 @@
         packs = [pack_y([values[k][f] for k in range(CH)]) for f in range(4)] + [pack_y(rho)]
         for f in range(5):
             YP[s, c + 1, f] = packs[f]
-        CP[0, s, c] = pack_high(packs[0], packs[1])
-        CP[1, s, c] = pack_low(packs[0], packs[1])
+        corner = jnp.where(first_half, packs[0], packs[1])
+        CP[0, s, c] = corner[4:]
+        CP[1, s, c] = corner[:4]
 
     def start_chunk(c, carry):
         states = [[QE[f, GHOST + c * CH + k] for f in range(5)] for k in range(CH)]
@@ -304,17 +305,19 @@
             copy.start()
         return carry
 
+    def ghost_primitives(c):
+        values = [primitives([QE[f, c * CH + k] for f in range(5)]) for k in range(CH)]
+        for s in range(2):
+            put(s, c, values)
+        return values
+
     def ghost_start():
         near = []
-        for c in (0, 1, chunks + 2, chunks + 3):
-            values = [primitives([QE[f, c * CH + k] for f in range(5)]) for k in range(CH)]
-            for s in range(2):
-                put(s, c, values)
-            if c in (1, chunks + 2):
-                near += values
-                e = 0 if c == 1 else chunks + 1
-                for f in (1, 2):
-                    YP[0, e, f] = pack_y([values[k][f] for k in range(CH)])
+        for e, c in ((0, 1), (chunks + 1, chunks + 2)):
+            values = ghost_primitives(c)
+            near += values
+            for f in (1, 2):
+                YP[0, e, f] = pack_y([values[k][f] for k in range(CH)])
         for i, f in enumerate((0, 2)):
             for k in range(4):
                 XSG[0, i, k] = pack_high(near[k][f], near[k + 4][f])
@@ -377,8 +380,11 @@
         return by_side([YN[way, s, c + 1, f] for way in y_sides])
 
     def corners(s, c):
-        pairs = [unpack_x(CN[way, 0, s, c], CN[way, 1, s, c]) for way in y_sides]
-        return [by_side([pair[f] for pair in pairs]) for f in range(2)]
+        pairs = [jnp.concatenate([CN[way, 1, s, c], CN[way, 0, s, c]], axis=0) for way in y_sides]
+        turned = [pltpu.roll(pair, 64, 1) for pair in pairs]
+        first = [jnp.where(first_half, pair, turn) for pair, turn in zip(pairs, turned, strict=True)]
+        second = [jnp.where(first_half, turn, pair) for pair, turn in zip(pairs, turned, strict=True)]
+        return [by_side(first), by_side(second)]
 
     def arrive(s, c):
         for copy in exchange(s, c):
@@ -514,15 +520,19 @@
         W[pl.ds(128, 128), part] = taps
 
     loads[0].wait()
-    for c in range(chunks):
-        start_chunk(c, 0)
     loads[1].wait()
+    ghost_start()
     loads[2].wait()
-    ghost_start()
+    start_chunk(0, 0)
     pl.semaphore_wait(barrier, len(neighbours))
     for copy in ghost_exchange():
         copy.start()
-    lax.fori_loop(0, chunks, send_chunk, 0)
+    send_chunk(0, 0)
+    for c in range(1, chunks):
+        start_chunk(c, 0)
+        send_chunk(c, 0)
+    ghost_primitives(0)
+    ghost_primitives(chunks + 3)
     for s in range(2):
         gradients_y(s)
         for c in range(chunks):
@@ -570,8 +580,8 @@
                 vmem(2, chunks + 4, SLOTS, rows=24),
                 vmem(2, chunks + 2, 5),
                 vmem(sides, 2, chunks + 2, 5),
-                vmem(2, 2, chunks),
-                vmem(sides, 2, 2, chunks),
+                vmem(2, 2, chunks, rows=4),
+                vmem(sides, 2, 2, chunks, rows=4),
                 vmem(4, planes + 8),
                 vmem(2, 2, 4),
                 vmem(2, 2, 4),

time: 24 us -> 23.7 us (0.987)
  Pallas kernels: 22.3 us -> 22 us
    pallas_call x1, Pallas kernels: 22.3 us -> 22 us  [body(): pl.pallas_call(functools.partial(kernel, nx, ny, chunks), out_shape=[pltp...]
where the time goes in v3:
time: 23.7 us; the launch traced here: 23.6 us
  Pallas kernels  22 us (93%)
  other arithmetic  0.91 us (4%)
  between operations  0.64 us (3%)
    pallas_call x1, Pallas kernels, body(): pl.pallas_call(functools.partial(kernel, nx, ny, chunks), out_shape=[pltp...  22 us
    add x1, other arithmetic, body(): return (state + section_b[1] * carried, carried)  0.91 us

profile of v3, /device:TPU:1, one launch (start us, length us, event | category | flops | bytes accessed | tf_op | source)
XLA Modules:
  0.0 23.6 jit_solution(6694778217930940111)
XLA Ops:
  0.6 22.0 %shard_map.50 = (f32[5,16,8,128]{3,2,1,0:T(8,128)S(1)}, f32[5,16,8,128]{3,2,1,0:T(8,128)S(1)}, f32[5,16,8,128]{3,2,1,0:T(8,128)S(1)}) custom-call(f32[5,16,8,128]{3,2,1,0:T(8,128)} %cons_hbm.1, f32[5,16,8,128]{3,2,1,0:T(8,128)} %reg_hbm.1, f32[5,16,8,128]{3,2,1,0:T(8,128)} %ghost_hbm.1), custom_call_target="tpu_custom_call" | custom-call | tf_op jit(solution)/shard_map/pallas_call | solution.py:572
  22.6 0.9 %multiply_add_fusion = (f32[5,16,8,128]{3,2,1,0:T(8,128)}, f32[5,16,8,128]{3,2,1,0:T(8,128)}) fusion(f32[5,16,8,128]{3,2,1,0:T(8,128)S(1)} %get-tuple-element.5, f32[5,16,8,128]{3,2,1,0:T(8,128)S(1)} %get-tuple-element.7, f32[5,16,8,128]{3,2,1,0:T(8,128)S(1)} %get-tuple-element.6), kind=kLoop, calls=%fused_computation | loop fusion | flops 409600 | bytes 1638400 | tf_op jit(solution)/shard_map/add | solution.py:616

commit v4 on v3

--- a/solution.py
+++ b/solution.py
@@ -36,7 +36,6 @@
     reg_hbm,
     ghost_hbm,
     state_out,
-    register_out,
     slope_out,
     QE,
     REG,
@@ -484,10 +483,10 @@
             for f in range(5):
                 slope = d_rows(FX, (f, w), 8) + add(RS[f, c], k, inner[CH * f + k]) + d_z(FZ, f, w + 4)
                 if s == 1:
-                    slope_out[f, w] = slope
+                    slope_out[f, w] = slope - (section_a[1] / time_step) * REG[f, w]
                     continue
                 register = section_a[0] * REG[f, w] - time_step * slope
-                register_out[f, w] = register
+                REG[f, w] = register
                 state = QE[f, z] + section_b[0] * register
                 QE[f, z] = state
                 state_out[f, w] = state
@@ -569,11 +568,11 @@
             return pltpu.VMEM(shape + (rows, columns), jnp.float32)
 
         dma = pltpu.SemaphoreType.DMA
-        state, old, slope = pl.pallas_call(
+        state, slope = pl.pallas_call(
             functools.partial(kernel, nx, ny, chunks),
-            out_shape=[pltpu.VMEM(conserved.shape, jnp.float32)] * 3,
+            out_shape=[pltpu.VMEM(conserved.shape, jnp.float32)] * 2,
             in_specs=[pl.BlockSpec(memory_space=pltpu.HBM)] * 3,
-            out_specs=[pl.BlockSpec(memory_space=pltpu.VMEM)] * 3,
+            out_specs=[pl.BlockSpec(memory_space=pltpu.VMEM)] * 2,
             scratch_shapes=[
                 vmem(5, planes + 2 * GHOST),
                 vmem(5, planes),
@@ -612,7 +611,7 @@
                 collective_id=0, has_side_effects=True, vmem_limit_bytes=60 * 1024 * 1024
             ),
         )(conserved, register, ghost_planes)
-        carried = section_a[1] * old - time_step * slope
+        carried = -time_step * slope
         return state + section_b[1] * carried, carried
 
     spec = P(None, None, "gx", "gy")

time: 23.7 us -> 23.7 us (level)
    add x1 -> x0, other arithmetic: 0.91 us -> none  [body(): return (state + section_b[1] * carried, carried)]
    mul x0 -> x1, other arithmetic: none -> 0.89 us  [body(): carried = -time_step * slope]
where the time goes in v4:
time: 23.7 us; the launch traced here: 23.5 us
  Pallas kernels  22 us (93%)
  other arithmetic  0.89 us (4%)
  between operations  0.64 us (3%)
    pallas_call x1, Pallas kernels, body(): pl.pallas_call(functools.partial(kernel, nx, ny, chunks), out_shape=[pltp...  22 us
    mul x1, other arithmetic, body(): carried = -time_step * slope  0.89 us

profile of v4, /device:TPU:1, one launch (start us, length us, event | category | flops | bytes accessed | tf_op | source)
XLA Modules:
  0.0 23.5 jit_solution(2865755723775684749)
XLA Ops:
  0.6 22.0 %shard_map.50 = (f32[5,16,8,128]{3,2,1,0:T(8,128)S(1)}, f32[5,16,8,128]{3,2,1,0:T(8,128)S(1)}) custom-call(f32[5,16,8,128]{3,2,1,0:T(8,128)} %cons_hbm.1, f32[5,16,8,128]{3,2,1,0:T(8,128)} %reg_hbm.1, f32[5,16,8,128]{3,2,1,0:T(8,128)} %ghost_hbm.1), custom_call_target="tpu_custom_call" | custom-call | tf_op jit(solution)/shard_map/pallas_call | solution.py:571
  22.6 0.9 %broadcast_multiply_fusion = (f32[5,16,8,128]{3,2,1,0:T(8,128)}, f32[5,16,8,128]{3,2,1,0:T(8,128)}) fusion(f32[5,16,8,128]{3,2,1,0:T(8,128)S(1)} %get-tuple-element.5, f32[5,16,8,128]{3,2,1,0:T(8,128)S(1)} %get-tuple-element.4), kind=kLoop, calls=%fused_computation.1 | loop fusion | flops 245760 | bytes 1310720 | tf_op jit(solution)/shard_map/mul | solution.py:614
